TPU v7x, 32 devices: a whole 2x2x4 slice. The times are simulated.
32 devices in a mesh: slide: 2 (over x), seq: 16 (over z, y, core).
Axes of the slice: x: 2, y: 2, z: 4, core: 2. Of those that a mesh axis runs over, the one named last changes fastest.
Arguments:
- tile_embed: bfloat16 [4096, 768], P(('slide', 'seq')), parts along dimension 0, may hold values from -8 to 8
- grad_output: bfloat16 [4096, 768], P(('slide', 'seq')), parts along dimension 0, may hold values from -6 to 6
- query_key_value_weight: bfloat16 [768, 2304], replicated, may hold values from -0.5 to 0.5
- conv_weight: float32 [9, 768], replicated, may hold values from -2.5 to 2.5
- neighbours: int32 [9, 4096], P(None, ('slide', 'seq')), parts along dimension 1, may hold values from -1 to 2047, as said below
Outputs:
- attended: bfloat16 [4096, 768], P(('slide', 'seq')), parts along dimension 0
- grad_tiles: bfloat16 [4096, 768], P(('slide', 'seq')), parts along dimension 0
- grad_conv: float32 [18, 768], P('slide'), parts along dimension 0
There are 2 independent parts, one for each index of `slide`. A program takes and returns all parts, laid end to end along the dimension named above; an argument that names none is the same for every part. Nothing has to cross between parts.
Inputs may be any that keep to these rules, and one draw needn't show every extreme that they name: Tiles are the tissue cells of a grid of 64 columns numbered in snake order. neighbours[k, i] is the tile at grid offset (k // 3 - 1, k % 3 - 1) from tile i, or -1 where that cell is outside the grid or background; neighbours[4, i] = i, and neighbours[8 - k, neighbours[k, i]] = i. Every neighbour lies within 127 positions of its tile, and some lies exactly 127 away.
All inputs are finite; a program needn't handle non-finite values.
Results may differ from a plain program's by a relative error of at most 0.012.
The roundings to bfloat16 on the way count: a program that leaves them out, or rounds other values in their place, can miss the bound.
Values may be sent and summed in bfloat16 or wider, within the bound.
A program may use at most 128 MiB of HBM per device.

v0:
```python
import jax
import jax.numpy as jnp
from jax import lax
from jax.sharding import PartitionSpec as P

MODEL_WIDTH = 768
HEAD_COUNT = 16
HEAD_SIZE = 48
DILATION_STEP = 4
KERNEL = 9
REACH = 127


def extended_2(shard, sides, width):
    for axis, dim in sides:
        count, length = (lax.axis_size(axis), shard.shape[dim])
        up = [(i, (i + 1) % count) for i in range(count - 1)]
        down = [(j, i) for i, j in up]
        last = lax.slice_in_dim(shard, length - width, length, axis=dim)
        leading = lax.slice_in_dim(shard, 0, width, axis=dim)
        before = lax.ppermute(last, axis, up)
        after = lax.ppermute(leading, axis, down)
        shard = jnp.concatenate([before, shard, after], axis=dim)
    return shard


def from_behind(value, axis, steps):
    count = lax.axis_size(axis)
    leading, last = (max(0, -steps), min(count, count - steps))
    return lax.ppermute(value, axis, [(source, source + steps) for source in range(leading, last)])


def select_dilated(full_result, item_count):
    each_group = HEAD_COUNT // DILATION_STEP
    five_value = full_result.reshape(
        item_count // DILATION_STEP, DILATION_STEP, each_group, DILATION_STEP, HEAD_SIZE
    )
    return jnp.stack(
        [
            five_value[:, residue_index, :, residue_index, :]
            for residue_index in range(DILATION_STEP)
        ],
        axis=2,
    ).reshape(item_count // DILATION_STEP, MODEL_WIDTH)


def spread_dilated(selected_rows):
    item_count = selected_rows.shape[0]
    five_value = selected_rows.reshape(
        item_count, 1, HEAD_COUNT // DILATION_STEP, DILATION_STEP, HEAD_SIZE
    )
    unit_vector = jnp.eye(DILATION_STEP, dtype=selected_rows.dtype).reshape(
        1, DILATION_STEP, 1, DILATION_STEP, 1
    )
    return (five_value * unit_vector).reshape(item_count * DILATION_STEP, MODEL_WIDTH)


def contract_last(left, right):
    return lax.dot_general(
        left, right, (((1,), (1,)), ((), ())), preferred_element_type=jnp.float32
    )


def contract_first(left, right):
    return lax.dot_general(
        left, right, (((0,), (0,)), ((), ())), preferred_element_type=jnp.float32
    )


def head_forward(items):
    queries, keys, values, douts = items
    scale = HEAD_SIZE ** (-0.5)
    scores = contract_last(queries, keys) * scale
    top = jnp.max(scores, axis=1, keepdims=True)
    log_total = top + jnp.log(jnp.sum(jnp.exp(scores - top), axis=1, keepdims=True))
    weights = jnp.exp(scores - log_total)
    weights_low = weights.astype(jnp.bfloat16)
    output = jnp.dot(weights_low, values, preferred_element_type=jnp.float32).astype(jnp.bfloat16)
    delta = jnp.sum(douts.astype(jnp.float32) * output.astype(jnp.float32), axis=1)
    dprob = contract_last(douts, values)
    dscore = (weights * (dprob - delta[:, None]) * scale).astype(jnp.bfloat16)
    grad_q = jnp.dot(dscore, keys, preferred_element_type=jnp.float32).astype(jnp.bfloat16)
    return (output, log_total[:, 0], delta, grad_q)


def head_keyside(items):
    query_piece, dout_piece, lse_piece, delta_piece, local_keys, local_values = items
    scale = HEAD_SIZE ** (-0.5)
    piece_scores = contract_last(query_piece, local_keys) * scale
    piece_weights = jnp.exp(piece_scores - lse_piece[:, None])
    value_part = contract_first(piece_weights.astype(jnp.bfloat16), dout_piece)
    piece_dprob = contract_last(dout_piece, local_values)
    piece_dscore = (piece_weights * (piece_dprob - delta_piece[:, None]) * scale).astype(
        jnp.bfloat16
    )
    key_part = contract_first(piece_dscore, query_piece)
    return (key_part, value_part)


def heads_lead(values, item_count):
    return jnp.transpose(values.reshape(item_count, HEAD_COUNT, HEAD_SIZE), (1, 0, 2))


def per_device(tile_embed, grad_output, query_key_value_weight, conv_weight, neighbours):
    count_of_rows = tile_embed.shape[0]
    partial_rows = count_of_rows // DILATION_STEP
    each_group = HEAD_COUNT // DILATION_STEP
    extended = extended_2(tile_embed, (("seq", 0),), REACH)
    valid = neighbours >= 0
    offset = lax.axis_index("seq") * count_of_rows - REACH
    local_index = jnp.where(valid, neighbours - offset, 0)
    valid_mask = valid.astype(jnp.float32)
    near_rows = [
        extended[local_index[k]].astype(jnp.float32) * valid_mask[k][:, None] for k in range(KERNEL)
    ]
    summed = tile_embed.astype(jnp.float32)
    for k in range(KERNEL):
        summed = summed + conv_weight[k][None, :] * near_rows[k]
    mixed_tiles = summed.astype(jnp.bfloat16)
    split_weights = query_key_value_weight.reshape(
        MODEL_WIDTH, 3, each_group, DILATION_STEP, HEAD_SIZE
    )
    per_residue_class = mixed_tiles.reshape(partial_rows, DILATION_STEP, MODEL_WIDTH)
    residue_weights = [
        split_weights[:, :, :, residue_index, :].reshape(MODEL_WIDTH, 3 * each_group * HEAD_SIZE)
        for residue_index in range(DILATION_STEP)
    ]
    projected = jnp.stack(
        [
            jnp.dot(
                per_residue_class[:, residue_index, :],
                residue_weights[residue_index],
                preferred_element_type=jnp.float32,
            )
            .astype(jnp.bfloat16)
            .reshape(partial_rows, 3, each_group, HEAD_SIZE)
            for residue_index in range(DILATION_STEP)
        ],
        axis=3,
    )
    query_sel = projected[:, 0].reshape(partial_rows, MODEL_WIDTH)
    key_sel = projected[:, 1].reshape(partial_rows, MODEL_WIDTH)
    value_sel = projected[:, 2].reshape(partial_rows, MODEL_WIDTH)
    dout_sel = select_dilated(grad_output, count_of_rows)
    key_all, value_all = (
        lax.all_gather(key_sel, "seq", axis=0, tiled=True),
        lax.all_gather(value_sel, "seq", axis=0, tiled=True),
    )
    total_keys = key_all.shape[0]
    output_h, lse_h, delta_h, grad_q_h = lax.map(
        head_forward,
        (
            heads_lead(query_sel, partial_rows),
            heads_lead(key_all, total_keys),
            heads_lead(value_all, total_keys),
            heads_lead(dout_sel, partial_rows),
        ),
    )
    grad_q = jnp.transpose(grad_q_h, (1, 0, 2)).reshape(partial_rows, MODEL_WIDTH)
    output_sel = jnp.transpose(output_h, (1, 0, 2)).reshape(partial_rows, MODEL_WIDTH)
    lse_all, delta_all = (
        lax.all_gather(lse_h.T, "seq", axis=0, tiled=True),
        lax.all_gather(delta_h.T, "seq", axis=0, tiled=True),
    )
    local_keys_h = heads_lead(key_sel, partial_rows)
    local_values_h = heads_lead(value_sel, partial_rows)
    query_piece = lax.all_gather(query_sel, "seq", axis=0, tiled=True)
    dout_piece = lax.all_gather(dout_sel, "seq", axis=0, tiled=True)
    item_count = query_piece.shape[0]
    key_part, value_part = lax.map(
        head_keyside,
        (
            heads_lead(query_piece, item_count),
            heads_lead(dout_piece, item_count),
            lse_all.T,
            delta_all.T,
            local_keys_h,
            local_values_h,
        ),
    )
    grad_k = (
        jnp.transpose(key_part, (1, 0, 2)).reshape(partial_rows, MODEL_WIDTH).astype(jnp.bfloat16)
    )
    grad_v = (
        jnp.transpose(value_part, (1, 0, 2)).reshape(partial_rows, MODEL_WIDTH).astype(jnp.bfloat16)
    )
    attended = spread_dilated(output_sel)
    gradient_list = (grad_q, grad_k, grad_v)
    dmixed_parts = []
    for residue_index in range(DILATION_STEP):
        stacked = jnp.stack(
            [
                group_index.reshape(partial_rows, each_group, DILATION_STEP, HEAD_SIZE)[
                    :, :, residue_index, :
                ]
                for group_index in gradient_list
            ],
            axis=1,
        )
        dmixed_parts.append(
            contract_last(
                stacked.reshape(partial_rows, 3 * each_group * HEAD_SIZE),
                residue_weights[residue_index],
            )
        )
    dmixed = jnp.stack(dmixed_parts, axis=1).reshape(count_of_rows, MODEL_WIDTH)
    conv_terms = jnp.stack([jnp.sum(dmixed * near_rows[k], axis=0) for k in range(KERNEL)])
    grad_conv = lax.psum(conv_terms, "seq")
    contrib = jnp.zeros((count_of_rows + 2 * REACH, MODEL_WIDTH), jnp.float32)
    for k in range(KERNEL):
        contrib = contrib.at[local_index[k]].add(
            conv_weight[k][None, :] * dmixed * valid_mask[k][:, None]
        )
    from_above = from_behind(contrib[:REACH], "seq", -1)
    from_below = from_behind(
        contrib[REACH + count_of_rows :].astype(jnp.bfloat16), "seq", 1
    ).astype(jnp.float32)
    total = dmixed + contrib[REACH : REACH + count_of_rows]
    total = total + jnp.pad(from_below, ((0, count_of_rows - REACH), (0, 0)))
    total = total + jnp.pad(from_above, ((count_of_rows - REACH, 0), (0, 0)))
    grad_tiles = total.astype(jnp.bfloat16)
    return (attended, grad_tiles, grad_conv)


def solution(mesh):
    placed = (
        P(("slide", "seq"), None),
        P(("slide", "seq"), None),
        P(),
        P(),
        P(None, ("slide", "seq")),
    )
    return jax.shard_map(
        per_device,
        mesh=mesh,
        in_specs=placed,
        out_specs=(P(("slide", "seq"), None), P(("slide", "seq"), None), P("slide", None)),
        check_vma=False,
    )
```

profile of v0, /device:TPU:0, one launch (start us, length us, event | category | flops | bytes accessed | tf_op | source)
XLA Modules:
  0.0 424.5 jit_solution(8289677350292391778)
XLA Ops:
  0.6 1.8 fusion.132
  3.8 3.7 collective-permute-start
  8.1 4.5 %copy.185 = bf16[768,2304]{0,1:T(8,128)(2,1)S(1)} copy(bf16[768,2304]{1,0:T(8,128)(2,1)} %param.11) | data formatting | bytes 7077888 | tf_op args[2]
  12.6 1.8 fusion.128
  18.6 25.6 %all_gather.22 = bf16[512,768]{1,0:T(8,128)(2,1)S(1)} all-gather(bf16[32,768]{1,0:T(8,128)(2,1)S(1)} %reshape.533), channel_id=1, replica_groups=mesh['slide'=2,'seq'=16] {'seq'}, dimensions={0}, use_global_device_ids=true | all-gather | bytes 835584 | tf_op jit(solution)/shard_map/all_gather | solution.py:168
  64.8 19.6 %all_gather.18 = bf16[512,768]{1,0:T(8,128)(2,1)S(1)} all-gather(bf16[32,768]{1,0:T(8,128)(2,1)S(1)} %reshape_squeeze.25), channel_id=1, replica_groups=mesh['slide'=2,'seq'=16] {'seq'}, dimensions={0}, use_global_device_ids=true | all-gather | bytes 835584 | tf_op jit(solution)/shard_map/all_gather | solution.py:146
  85.6 21.3 %all_gather.19 = bf16[512,768]{1,0:T(8,128)(2,1)S(1)} all-gather(bf16[32,768]{1,0:T(8,128)(2,1)S(1)} %copy-done.26), channel_id=1, replica_groups=mesh['slide'=2,'seq'=16] {'seq'}, dimensions={0}, use_global_device_ids=true | all-gather | bytes 835584 | tf_op jit(solution)/shard_map/all_gather | solution.py:147
  108.0 86.8 %while.28 = (s32[]{:T(128)}, bf16[16,32,48]{2,1,0:T(8,128)(2,1)}, f32[16,32]{1,0:T(8,128)S(1)}, f32[16,32]{1,0:T(8,128)S(1)}, bf16[16,32,48]{2,1,0:T(8,128)(2,1)...) while((s32[]{:T(128)}, bf16[16,32,48]{2,1,0:T(8,128)(2,1)}, ...), condition=%wide.region_4.5_spmd, body=%wide.region_0.4_spmd.sunk | while | flops 6480834 | bytes 506753 | solution.py:150
  111.8 1.7 fusion.167
  117.2 1.7 fusion.167
  122.6 1.7 fusion.167
  128.1 1.7 fusion.167
  131.0 1.6 bitcast_dynamic-update-slice_fusion.2
  133.5 1.7 fusion.167
  138.9 1.7 fusion.167
  144.3 1.7 fusion.167
  149.7 1.7 fusion.167
  152.7 1.6 bitcast_dynamic-update-slice_fusion.2
  155.2 1.7 fusion.167
  160.6 1.7 fusion.167
  166.0 1.7 fusion.167
  168.9 1.6 bitcast_dynamic-update-slice_fusion.2
  171.4 1.7 fusion.167
  176.8 1.7 fusion.167
  182.2 1.7 fusion.167
  185.2 1.6 bitcast_dynamic-update-slice_fusion.2
  187.7 1.7 fusion.167
  193.1 1.7 fusion.167
  194.8 1.6 copy.202
  196.4 19.6 %all_gather.20 = bf16[512,768]{1,0:T(8,128)(2,1)S(1)} all-gather(bf16[32,768]{1,0:T(8,128)(2,1)S(1)} %reshape_squeeze.27), channel_id=1, replica_groups=mesh['slide'=2,'seq'=16] {'seq'}, dimensions={0}, use_global_device_ids=true | all-gather | bytes 835584 | tf_op jit(solution)/shard_map/all_gather | solution.py:167
  217.2 19.3 %all-gather = f32[16,32,16]{1,2,0:T(8,128)S(1)} all-gather(f32[1,32,16]{1,2,0:T(8,128)S(1)} %bitcast.357), channel_id=1, replica_groups=mesh['slide'=2,'seq'=16] {'seq'}, dimensions={0}, use_global_device_ids=true | all-gather | bytes 34816 | tf_op jit(solution)/shard_map/all_gather | solution.py:162
  236.6 17.8 %all-gather.1 = f32[16,32,16]{1,2,0:T(8,128)S(1)} all-gather(f32[1,32,16]{1,2,0:T(8,128)S(1)} %bitcast.358), channel_id=1, replica_groups=mesh['slide'=2,'seq'=16] {'seq'}, dimensions={0}, use_global_device_ids=true | all-gather | bytes 34816 | tf_op jit(solution)/shard_map/all_gather | solution.py:163
  254.6 66.9 %while.29 = (s32[]{:T(128)}, bf16[16,32,48]{2,1,0:T(8,128)(2,1)}, bf16[16,32,48]{2,1,0:T(8,128)(2,1)}, bf16[16,512,48]{1,2,0:T(8,128)(2,1)}, bf16[16,32,48]{2,1,...) while((s32[]{:T(128)}, bf16[16,32,48]{2,1,0:T(8,128)(2,1)}, ...), condition=%wide.region_6.7_spmd, body=%wide.region_5.6_spmd.sunk | while | flops 6406146 | bytes 458865 | solution.py:170
  255.5 1.7 fusion.176
  259.7 1.7 fusion.176
  263.9 1.7 fusion.176
  268.1 1.7 fusion.176
  272.3 1.7 fusion.176
  276.5 1.7 fusion.176
  280.6 1.7 fusion.176
  284.8 1.7 fusion.176
  289.0 1.7 fusion.176
  293.2 1.7 fusion.176
  297.4 1.7 fusion.176
  301.6 1.7 fusion.176
  305.7 1.7 fusion.176
  309.9 1.7 fusion.176
  314.1 1.7 fusion.176
  318.3 1.7 fusion.176
  326.7 1.6 reshape.538
  328.4 1.7 convolution_bitcast_fusion.1
  334.1 1.9 scatter_custom_fusion
  336.1 2.1 scatter_custom_fusion.1
  338.2 2.1 scatter_custom_fusion.2
  340.3 2.1 scatter_custom_fusion.3
  342.5 2.1 scatter_custom_fusion.4
  344.6 2.1 scatter_custom_fusion.5
  346.6 2.1 scatter_custom_fusion.6
  348.7 2.1 scatter_custom_fusion.7
  350.8 2.1 scatter_custom_fusion.8
  358.1 3.0 collective-permute-start.2
  361.2 1.6 multiply_reduce_fusion.1
  363.0 59.7 %psum.7 = f32[9,768]{1,0:T(8,128)} all-reduce(f32[9,768]{1,0:T(8,128)S(1)} %stack.83), channel_id=1, replica_groups=mesh['slide'=2,'seq'=16] {'seq'}, use_global_device_ids=true, to_apply=%region_25.26 | all-reduce | flops 6912 | bytes 55296 | tf_op jit(solution)/shard_map/psum | solution.py:208
  422.7 1.8 fusion.71
  (419 shorter events, 136.9 us)
Async XLA Ops:
  2.5 43.1 %collective-permute-start.1 = (bf16[127,768]{1,0:T(8,128)(2,1)}, bf16[127,768]{1,0:T(8,128)(2,1)}, u32[]{:S(2)}, u32[]{:S(2)}) collective-permute-start(bf16[127,768]{1,0:T(8,128)(2,1)} %get-tuple-element.273), channel_id=1, source_target_pairs={{1,0},{2,1},{3,2},{4,3},{5,4},{6,5},{7,6},{8,7},{9,8},{10,9},{11,1... | collective-permute-start | bytes 585224 | tf_op jit(solution)/shard_map/ppermute | solution.py:22
  3.8 41.8 %collective-permute-start = (bf16[127,768]{1,0:T(8,128)(2,1)}, bf16[127,768]{1,0:T(8,128)(2,1)}, u32[]{:S(2)}, u32[]{:S(2)}) collective-permute-start(bf16[127,768]{1,0:T(8,128)(2,1)} %get-tuple-element.272), channel_id=1, source_target_pairs={{0,1},{1,2},{2,3},{3,4},{4,5},{5,6},{6,7},{7,8},{8,9},{9,10},{10,1... | collective-permute-start | bytes 585224 | tf_op jit(solution)/shard_map/ppermute | solution.py:21
  14.5 4.1 copy-start.73
  14.5 30.9 %copy-start.65 = (s32[128]{0:T(128)}, s32[128]{0:T(128)S(1)}, u32[]{:S(2)}) copy-start(s32[128]{0:T(128)S(1)} %get-tuple-element.296) | copy-start | bytes 1540
  14.5 30.9 %copy-start.66 = (s32[128]{0:T(128)}, s32[128]{0:T(128)S(1)}, u32[]{:S(2)}) copy-start(s32[128]{0:T(128)S(1)} %get-tuple-element.297) | copy-start | bytes 1540
  14.5 30.9 %copy-start.67 = (s32[128]{0:T(128)}, s32[128]{0:T(128)S(1)}, u32[]{:S(2)}) copy-start(s32[128]{0:T(128)S(1)} %get-tuple-element.298) | copy-start | bytes 1540
  14.5 30.9 %copy-start.68 = (s32[128]{0:T(128)}, s32[128]{0:T(128)S(1)}, u32[]{:S(2)}) copy-start(s32[128]{0:T(128)S(1)} %get-tuple-element.299) | copy-start | bytes 1540
  14.5 30.9 %copy-start.69 = (s32[128]{0:T(128)}, s32[128]{0:T(128)S(1)}, u32[]{:S(2)}) copy-start(s32[128]{0:T(128)S(1)} %get-tuple-element.300) | copy-start | bytes 1540
  14.5 30.9 %copy-start.70 = (s32[128]{0:T(128)}, s32[128]{0:T(128)S(1)}, u32[]{:S(2)}) copy-start(s32[128]{0:T(128)S(1)} %get-tuple-element.301) | copy-start | bytes 1540
  14.5 30.9 %copy-start.71 = (s32[128]{0:T(128)}, s32[128]{0:T(128)S(1)}, u32[]{:S(2)}) copy-start(s32[128]{0:T(128)S(1)} %get-tuple-element.302) | copy-start | bytes 1540
  14.5 30.9 %copy-start.72 = (s32[128]{0:T(128)}, s32[128]{0:T(128)S(1)}, u32[]{:S(2)}) copy-start(s32[128]{0:T(128)S(1)} %get-tuple-element.303) | copy-start | bytes 1540
  15.7 39.0 %copy-start.34 = (f32[768]{0:T(1024)}, f32[768]{0:T(1024)S(1)}, u32[]{:S(2)}) copy-start(f32[768]{0:T(1024)S(1)} %get-tuple-element.209) | copy-start | bytes 9220
  15.7 39.0 %copy-start.36 = (f32[768]{0:T(1024)}, f32[768]{0:T(1024)S(1)}, u32[]{:S(2)}) copy-start(f32[768]{0:T(1024)S(1)} %get-tuple-element.210) | copy-start | bytes 9220
  15.7 39.0 %copy-start.38 = (f32[768]{0:T(1024)}, f32[768]{0:T(1024)S(1)}, u32[]{:S(2)}) copy-start(f32[768]{0:T(1024)S(1)} %get-tuple-element.211) | copy-start | bytes 9220
  15.7 39.0 %copy-start.40 = (f32[768]{0:T(1024)}, f32[768]{0:T(1024)S(1)}, u32[]{:S(2)}) copy-start(f32[768]{0:T(1024)S(1)} %get-tuple-element.212) | copy-start | bytes 9220
  15.7 39.0 %copy-start.42 = (f32[768]{0:T(1024)}, f32[768]{0:T(1024)S(1)}, u32[]{:S(2)}) copy-start(f32[768]{0:T(1024)S(1)} %get-tuple-element.206) | copy-start | bytes 9220
  18.5 27.0 %copy-start.5 = (bf16[128,768]{1,0:T(8,128)(2,1)S(1)}, bf16[128,768]{1,0:T(8,128)(2,1)}, u32[]{:S(2)}) copy-start(bf16[128,768]{1,0:T(8,128)(2,1)} %param.9) | copy-start | bytes 589828
  45.5 9.2 %copy-start.45 = (f32[128]{0:T(128)}, f32[128]{0:T(128)S(1)}, u32[]{:S(2)}) copy-start(f32[128]{0:T(128)S(1)} %get-tuple-element.286) | copy-start | bytes 1540
  45.5 9.2 %copy-start.47 = (f32[128]{0:T(128)}, f32[128]{0:T(128)S(1)}, u32[]{:S(2)}) copy-start(f32[128]{0:T(128)S(1)} %get-tuple-element.287) | copy-start | bytes 1540
  45.5 9.2 %copy-start.49 = (f32[128]{0:T(128)}, f32[128]{0:T(128)S(1)}, u32[]{:S(2)}) copy-start(f32[128]{0:T(128)S(1)} %get-tuple-element.288) | copy-start | bytes 1540
  45.5 9.2 %copy-start.51 = (f32[128]{0:T(128)}, f32[128]{0:T(128)S(1)}, u32[]{:S(2)}) copy-start(f32[128]{0:T(128)S(1)} %get-tuple-element.289) | copy-start | bytes 1540
  45.5 9.2 %copy-start.53 = (f32[128]{0:T(128)}, f32[128]{0:T(128)S(1)}, u32[]{:S(2)}) copy-start(f32[128]{0:T(128)S(1)} %get-tuple-element.290) | copy-start | bytes 1540
  45.5 9.2 %copy-start.55 = (f32[128]{0:T(128)}, f32[128]{0:T(128)S(1)}, u32[]{:S(2)}) copy-start(f32[128]{0:T(128)S(1)} %get-tuple-element.291) | copy-start | bytes 1540
  45.5 9.2 %copy-start.57 = (f32[128]{0:T(128)}, f32[128]{0:T(128)S(1)}, u32[]{:S(2)}) copy-start(f32[128]{0:T(128)S(1)} %get-tuple-element.292) | copy-start | bytes 1540
  45.5 9.2 %copy-start.59 = (f32[128]{0:T(128)}, f32[128]{0:T(128)S(1)}, u32[]{:S(2)}) copy-start(f32[128]{0:T(128)S(1)} %get-tuple-element.293) | copy-start | bytes 1540
  45.6 9.2 %copy-start.61 = (f32[128]{0:T(128)}, f32[128]{0:T(128)S(1)}, u32[]{:S(2)}) copy-start(f32[128]{0:T(128)S(1)} %get-tuple-element.294) | copy-start | bytes 1540
  47.6 7.2 %copy-start.6 = (bf16[128,768]{1,0:T(8,128)(2,1)}, bf16[128,768]{1,0:T(8,128)(2,1)S(1)}, u32[]{:S(2)}) copy-start(bf16[128,768]{1,0:T(8,128)(2,1)S(1)} %gather_fusion.8) | copy-start | bytes 589828
  48.5 6.3 %copy-start.8 = (bf16[128,768]{1,0:T(8,128)(2,1)}, bf16[128,768]{1,0:T(8,128)(2,1)S(1)}, u32[]{:S(2)}) copy-start(bf16[128,768]{1,0:T(8,128)(2,1)S(1)} %gather_fusion.7) | copy-start | bytes 589828
  49.4 5.4 %copy-start.10 = (bf16[128,768]{1,0:T(8,128)(2,1)}, bf16[128,768]{1,0:T(8,128)(2,1)S(1)}, u32[]{:S(2)}) copy-start(bf16[128,768]{1,0:T(8,128)(2,1)S(1)} %gather_fusion.6) | copy-start | bytes 589828
  50.2 4.6 %copy-start.12 = (bf16[128,768]{1,0:T(8,128)(2,1)}, bf16[128,768]{1,0:T(8,128)(2,1)S(1)}, u32[]{:S(2)}) copy-start(bf16[128,768]{1,0:T(8,128)(2,1)S(1)} %gather_fusion.5) | copy-start | bytes 589828
  51.1 3.7 copy-start.14
  52.0 2.8 copy-start.16
  52.9 2.0 copy-start.18
  56.5 2.4 copy-start.1
  56.9 2.0 copy-start.25
  57.2 2.4 copy-start
  57.2 2.4 copy-start.24
  321.5 6.9 %copy-start.4 = (bf16[768,3,4,1,48]{0,4,3,2,1:T(8,128)(2,1)S(1)}, bf16[768,3,4,1,48]{0,4,3,2,1:T(8,128)(2,1)}, u32[]{:S(2)}) copy-start(bf16[768,3,4,1,48]{0,4,3,2,1:T(8,128)(2,1)} %get-tuple-element.258) | copy-start | bytes 2654212
  328.4 3.3 copy-start.33
  330.1 2.1 copy-start.30
  330.1 2.2 copy-start.31
  330.1 2.2 copy-start.32
  333.7 2.3 copy-start.41
  333.7 2.3 copy-start.62
  336.0 2.1 copy-start.39
  336.0 2.1 copy-start.60
  338.2 2.1 copy-start.37
  338.2 2.1 copy-start.58
  340.3 2.1 copy-start.35
  340.3 2.1 copy-start.56
  342.4 2.1 copy-start.54
  344.5 2.1 copy-start.52
  346.6 2.1 copy-start.50
  348.7 2.1 copy-start.48
  350.8 4.2 copy-start.74
  352.9 8.2 %copy-start.7 = (bf16[128,768]{1,0:T(8,128)(2,1)S(1)}, bf16[128,768]{1,0:T(8,128)(2,1)}, u32[]{:S(2)}) copy-start(bf16[128,768]{1,0:T(8,128)(2,1)} %copy-done.6) | copy-start | bytes 589828
  352.9 8.2 %copy-start.9 = (bf16[128,768]{1,0:T(8,128)(2,1)S(1)}, bf16[128,768]{1,0:T(8,128)(2,1)}, u32[]{:S(2)}) copy-start(bf16[128,768]{1,0:T(8,128)(2,1)} %copy-done.8) | copy-start | bytes 589828
  352.9 8.2 %copy-start.11 = (bf16[128,768]{1,0:T(8,128)(2,1)S(1)}, bf16[128,768]{1,0:T(8,128)(2,1)}, u32[]{:S(2)}) copy-start(bf16[128,768]{1,0:T(8,128)(2,1)} %copy-done.10) | copy-start | bytes 589828
  353.0 8.2 %copy-start.13 = (bf16[128,768]{1,0:T(8,128)(2,1)S(1)}, bf16[128,768]{1,0:T(8,128)(2,1)}, u32[]{:S(2)}) copy-start(bf16[128,768]{1,0:T(8,128)(2,1)} %copy-done.12) | copy-start | bytes 589828
  353.0 8.2 %copy-start.15 = (bf16[128,768]{1,0:T(8,128)(2,1)S(1)}, bf16[128,768]{1,0:T(8,128)(2,1)}, u32[]{:S(2)}) copy-start(bf16[128,768]{1,0:T(8,128)(2,1)} %copy-done.14) | copy-start | bytes 589828
  353.0 8.2 %copy-start.17 = (bf16[128,768]{1,0:T(8,128)(2,1)S(1)}, bf16[128,768]{1,0:T(8,128)(2,1)}, u32[]{:S(2)}) copy-start(bf16[128,768]{1,0:T(8,128)(2,1)} %copy-done.16) | copy-start | bytes 589828
  353.0 8.2 %copy-start.19 = (bf16[128,768]{1,0:T(8,128)(2,1)S(1)}, bf16[128,768]{1,0:T(8,128)(2,1)}, u32[]{:S(2)}) copy-start(bf16[128,768]{1,0:T(8,128)(2,1)} %copy-done.18) | copy-start | bytes 589828
  353.8 69.0 %collective-permute-start.3 = (f32[127,768]{1,0:T(8,128)}, f32[127,768]{1,0:T(8,128)}, u32[]{:S(2)}, u32[]{:S(2)}) collective-permute-start(f32[127,768]{1,0:T(8,128)} %slice.329), channel_id=1, source_target_pairs={{1,0},{2,1},{3,2},{4,3},{5,4},{6,5},{7,6},{8,7},{9,8},{10,9},{11,1... | collective-permute-start | bytes 1170440 | tf_op jit(solution)/shard_map/ppermute | solution.py:30
  358.1 64.6 %collective-permute-start.2 = (bf16[127,768]{1,0:T(8,128)(2,1)}, bf16[127,768]{1,0:T(8,128)(2,1)S(1)}, u32[]{:S(2)}, u32[]{:S(2)}) collective-permute-start(bf16[127,768]{1,0:T(8,128)(2,1)} %slice.383), channel_id=1, source_target_pairs={{0,1},{1,2},{2,3},{3,4},{4,5},{5,6},{6,7},{7,8},{8,9},{9,10},{10,1... | collective-permute-start | bytes 585224 | tf_op jit(solution)/shard_map/ppermute | solution.py:30
  (15 other events, 16.9 us)
where the time goes:
time: 432 us; the launch traced here: 424 us
  blocking collectives  183 us (42%)
  matrix products  141 us (33%)
  local copies, waits for them, and re-layouts  45.1 us (10%)
  other arithmetic  43.9 us (10%)
  starting transfers between devices  9.32 us (2%)
    psum x1, blocking collectives, per_device(): grad_conv = lax.psum(conv_terms, 'seq')  59.7 us
    dot_general x32, matrix products, contract_first(): lax.dot_general(left, right, (((0,), (0,)), ((), ())), preferred_element_...  51.4 us
    dot_general x36, matrix products, contract_last(): lax.dot_general(left, right, (((1,), (1,)), ((), ())), preferred_element_...  34.3 us
    dot_general x16, matrix products, head_forward(): jnp.dot(dscore, keys, preferred_element_type=jnp.float32)  27 us
    dot_general x16, matrix products, head_forward(): jnp.dot(weights_low, values, preferred_element_type=jnp.float32)  25.6 us
    all_gather x1, blocking collectives, per_device(): dout_piece = lax.all_gather(dout_sel, 'seq', axis=0, tiled=True)  25.6 us
    all_gather x1, blocking collectives, per_device(): lax.all_gather(value_sel, 'seq', axis=0, tiled=True)  21.3 us
    all_gather x1, blocking collectives, per_device(): lax.all_gather(key_sel, 'seq', axis=0, tiled=True)  19.6 us
  transfers between devices with their start and end apart: 4, of which 0 were waited for; matrix products, arithmetic and copies ran while one was open for 4% of the time, Pallas kernels for 0%

commit v1 on v0

--- a/solution.py
+++ b/solution.py
@@ -1,6 +1,10 @@
+import functools
+
 import jax
 import jax.numpy as jnp
 from jax import lax
+from jax.experimental import pallas as pl
+from jax.experimental.pallas import tpu as pltpu
 from jax.sharding import PartitionSpec as P
 
 MODEL_WIDTH = 768
@@ -222,6 +226,399 @@
     return (attended, grad_tiles, grad_conv)
 
 
+ROWS = 128
+PART = ROWS // DILATION_STEP
+PACKED = 48
+LANES = 128
+CHUNKS = MODEL_WIDTH // LANES
+VMEM_BYTES = 56 * 1024 * 1024
+
+
+def bf16_dot(left, right):
+    return jnp.dot(left, right, preferred_element_type=jnp.float32)
+
+
+def one_hot(column, positions):
+    return jnp.where(column == positions, 1.0, 0.0).astype(jnp.bfloat16)
+
+
+def remote(source, target, send_sem, recv_sem, peer):
+    return pltpu.make_async_remote_copy(
+        src_ref=source,
+        dst_ref=target,
+        send_sem=send_sem,
+        recv_sem=recv_sem,
+        device_id={"seq": peer},
+        device_id_type=pl.DeviceIdType.MESH,
+    )
+
+
+def slide_kernel(
+    n,
+    tile_ref,
+    dout_ref,
+    weight_hbm,
+    conv_ref,
+    near_ref,
+    attended_ref,
+    tiles_ref,
+    taps_ref,
+    weight,
+    near_pad,
+    columns,
+    columns_perm,
+    halo,
+    gathered_own,
+    gathered,
+    hot_own,
+    hot_halo,
+    back_own,
+    back_halo,
+    dout_perm,
+    heads_out,
+    heads_in,
+    grads_out,
+    grads_in,
+    split,
+    back_rows,
+    tap_part,
+    tap_in,
+    tap_all,
+    weight_sem,
+    halo_s,
+    halo_r,
+    heads_s,
+    heads_r,
+    grads_s,
+    grads_r,
+    back_s,
+    back_r,
+    tap_s,
+    tap_r,
+    all_s,
+    all_r,
+):
+    me = lax.axis_index("seq")
+    load_weight = pltpu.make_async_copy(weight_hbm, weight, weight_sem)
+    load_weight.start()
+
+    barrier = pltpu.get_barrier_semaphore()
+
+    @pl.loop(1, n)
+    def _(step):
+        pl.semaphore_signal(
+            barrier,
+            inc=1,
+            device_id={"seq": lax.rem(me + step, n)},
+            device_id_type=pl.DeviceIdType.MESH,
+        )
+
+    near = near_ref[...]
+    near_pad[...] = jnp.full((LANES, ROWS), -1, jnp.int32)
+    near_pad[0:KERNEL, :] = jnp.where(near >= 0, near - (me - 1) * ROWS, -1)
+    columns[...] = near_pad[...].T
+    for r in range(DILATION_STEP):
+        columns_perm[r * PART : (r + 1) * PART, :] = columns[pl.ds(r, PART, stride=DILATION_STEP), :]
+    lane = lax.broadcasted_iota(jnp.int32, (ROWS, ROWS), 1)
+    row = lax.broadcasted_iota(jnp.int32, (ROWS, ROWS), 0)
+    tile_of_lane = (lane % PART) * DILATION_STEP + lane // PART
+    tile_of_row = (row % PART) * DILATION_STEP + row // PART
+    for k in range(KERNEL):
+        column = columns_perm[:, k : k + 1]
+        rows = slice(k * ROWS, (k + 1) * ROWS)
+        hot_own[rows, :] = one_hot(column, lane + ROWS)
+        hot_halo[rows, 0:ROWS] = one_hot(column, lane)
+        hot_halo[rows, ROWS : 2 * ROWS] = one_hot(column, lane + 2 * ROWS)
+    to_perm = one_hot(tile_of_row, lane)
+    dout_perm[...] = bf16_dot(to_perm, dout_ref[...]).astype(jnp.bfloat16)
+
+    pl.semaphore_wait(barrier, n - 1)
+
+    def exchange(source, target, send_sem, recv_sem):
+        up = remote(source, target.at[pl.ds(0, ROWS)], send_sem.at[0], recv_sem.at[0], me + 1)
+        down = remote(source, target.at[pl.ds(ROWS, ROWS)], send_sem.at[1], recv_sem.at[1], me - 1)
+        return up, down
+
+    def start_exchange(copies):
+        pl.when(me < n - 1)(copies[0].start)
+        pl.when(me > 0)(copies[1].start)
+
+    def arrive_exchange(copies):
+        pl.when(me > 0)(copies[0].wait_recv)
+        pl.when(me < n - 1)(copies[1].wait_recv)
+
+    def finish_exchange(copies):
+        pl.when(me < n - 1)(copies[0].wait_send)
+        pl.when(me > 0)(copies[1].wait_send)
+
+    def clear_ends(target):
+        @pl.when(me == 0)
+        def _():
+            target[0:ROWS, :] = jnp.zeros((ROWS, MODEL_WIDTH), jnp.bfloat16)
+
+        @pl.when(me == n - 1)
+        def _():
+            target[ROWS : 2 * ROWS, :] = jnp.zeros((ROWS, MODEL_WIDTH), jnp.bfloat16)
+
+    tile_copies = exchange(tile_ref, halo, halo_s, halo_r)
+    start_exchange(tile_copies)
+    clear_ends(halo)
+    clear_ends(back_rows)
+    gathered_own[...] = bf16_dot(hot_own[...], tile_ref[...])
+    for h in range(HEAD_COUNT):
+        r = h % DILATION_STEP
+        piece = dout_perm[r * PART : (r + 1) * PART, h * HEAD_SIZE : (h + 1) * HEAD_SIZE]
+        heads_out[h, PART:PACKED, 32:80] = piece[0:16]
+        heads_out[h, PART:PACKED, 80:128] = piece[16:32]
+    for k in range(KERNEL):
+        column = columns[:, k : k + 1]
+        rows = slice(k * ROWS, (k + 1) * ROWS)
+        own = one_hot(column, tile_of_lane + ROWS)
+        back_own[rows, 0:ROWS] = own
+        back_own[rows, ROWS : 2 * ROWS] = own
+        back_halo[rows, 0:ROWS] = one_hot(column, tile_of_lane)
+        back_halo[rows, ROWS : 2 * ROWS] = one_hot(column, tile_of_lane + 2 * ROWS)
+
+    arrive_exchange(tile_copies)
+    gathered[...] = (gathered_own[...] + bf16_dot(hot_halo[...], halo[...])).astype(jnp.bfloat16)
+
+    def tap_rows(k):
+        return gathered[k * ROWS : (k + 1) * ROWS, :].astype(jnp.float32)
+
+    summed = tap_rows(KERNEL // 2)
+    for k in range(KERNEL):
+        summed = summed + conv_ref[k : k + 1, :] * tap_rows(k)
+    mixed = summed.astype(jnp.bfloat16)
+
+    load_weight.wait()
+    projected = [
+        bf16_dot(mixed, weight[:, s * MODEL_WIDTH : (s + 1) * MODEL_WIDTH]).astype(jnp.bfloat16)
+        for s in range(3)
+    ]
+    for h in range(HEAD_COUNT):
+        r = h % DILATION_STEP
+        q, k, v = [
+            x[r * PART : (r + 1) * PART, h * HEAD_SIZE : (h + 1) * HEAD_SIZE] for x in projected
+        ]
+        heads_out[h, 0:PART, :] = jnp.concatenate([q, k, v[:, 0:32]], axis=1)
+        heads_out[h, PART:PACKED, 0:16] = v[0:16, 32:48]
+        heads_out[h, PART:PACKED, 16:32] = v[16:32, 32:48]
+
+    def all_to_all(source, target, send_sem, recv_sem):
+        @pl.loop(1, n)
+        def _(step):
+            peer = lax.rem(me + step, n)
+            remote(
+                source.at[peer], target.at[me], send_sem.at[peer], recv_sem.at[me], peer
+            ).start()
+
+        target[me] = source[me]
+
+        @pl.loop(1, n)
+        def _(step):
+            peer = lax.rem(me + n - step, n)
+            remote(
+                source.at[peer], target.at[peer], send_sem.at[peer], recv_sem.at[peer], peer
+            ).wait_recv()
+
+    def finish_all_to_all(source, target, send_sem, recv_sem):
+        @pl.loop(1, n)
+        def _(step):
+            peer = lax.rem(me + step, n)
+            remote(
+                source.at[peer], target.at[me], send_sem.at[peer], recv_sem.at[me], peer
+            ).wait_send()
+
+    all_to_all(heads_out, heads_in, heads_s, heads_r)
+
+    keys_total = n * PART
+    front = heads_in[:, 0:PART, :].reshape(keys_total, LANES)
+    rest = heads_in[:, PART:PACKED, :]
+    q = front[:, 0:48]
+    k = front[:, 48:96]
+    v_tail = jnp.concatenate([rest[:, :, 0:16], rest[:, :, 16:32]], axis=1).reshape(keys_total, 16)
+    v = jnp.concatenate([front[:, 96:128], v_tail], axis=1)
+    do = jnp.concatenate([rest[:, :, 32:80], rest[:, :, 80:128]], axis=1).reshape(keys_total, 48)
+    scale = HEAD_SIZE ** (-0.5)
+    scores = contract_last(k, q) * scale
+    top = jnp.max(scores, axis=0, keepdims=True)
+    grown = jnp.exp(scores - top)
+    prob = grown * (1.0 / jnp.sum(grown, axis=0, keepdims=True))
+    prob_low = prob.astype(jnp.bfloat16)
+    out_t = bf16_dot(v.T, prob_low).astype(jnp.bfloat16)
+    delta = jnp.sum(
+        do.T.astype(jnp.float32) * out_t.astype(jnp.float32), axis=0, keepdims=True
+    )
+    dprob = contract_last(v, do)
+    dscore = (prob * (dprob - delta) * scale).astype(jnp.bfloat16)
+    out = out_t.T
+    dq = bf16_dot(k.T, dscore).astype(jnp.bfloat16).T
+    dk = bf16_dot(dscore, q).astype(jnp.bfloat16)
+    dv = bf16_dot(prob_low, do).astype(jnp.bfloat16)
+    grads_out[:, 0:PART, :] = jnp.concatenate([out, dq, dk[:, 0:32]], axis=1).reshape(
+        n, PART, LANES
+    )
+    dk_tail = dk[:, 32:48].reshape(n, PART, 16)
+    dv_rows = dv.reshape(n, PART, HEAD_SIZE)
+    grads_out[:, PART:PACKED, :] = jnp.concatenate(
+        [dk_tail[:, 0:16], dk_tail[:, 16:32], dv_rows[:, 0:16], dv_rows[:, 16:32]], axis=2
+    )
+    all_to_all(grads_out, grads_in, grads_s, grads_r)
+
+    blank = jnp.zeros((PART, HEAD_SIZE), jnp.bfloat16)
+    grown_rows = [[], [], [], []]
+    for r in range(DILATION_STEP):
+        lists = [[], [], [], []]
+        for h in range(HEAD_COUNT):
+            if h % DILATION_STEP != r:
+                for entry in lists:
+                    entry.append(blank)
+                continue
+            x = grads_in[h, 0:PART, :]
+            y = grads_in[h, PART:PACKED, :]
+            lists[0].append(x[:, 0:48])
+            lists[1].append(x[:, 48:96])
+            tail = jnp.concatenate([y[:, 0:16], y[:, 16:32]], axis=0)
+            lists[2].append(jnp.concatenate([x[:, 96:128], tail], axis=1))
+            lists[3].append(jnp.concatenate([y[:, 32:80], y[:, 80:128]], axis=0))
+        for s in range(4):
+            grown_rows[s].append(jnp.concatenate(lists[s], axis=1))
+    out_perm, dq_perm, dk_perm, dv_perm = [jnp.concatenate(x, axis=0) for x in grown_rows]
+    dmixed = jnp.zeros((ROWS, MODEL_WIDTH), jnp.float32)
+    for s, part in enumerate((dq_perm, dk_perm, dv_perm)):
+        dmixed = dmixed + contract_last(part, weight[:, s * MODEL_WIDTH : (s + 1) * MODEL_WIDTH])
+    high = dmixed.astype(jnp.bfloat16)
+    split[0:ROWS, :] = high
+    split[ROWS : 2 * ROWS, :] = (dmixed - high.astype(jnp.float32)).astype(jnp.bfloat16)
+    back_copies = exchange(split.at[pl.ds(0, ROWS)], back_rows, back_s, back_r)
+    start_exchange(back_copies)
+
+    tap_part[...] = jnp.zeros_like(tap_part)
+    for k in range(KERNEL):
+        term = jnp.sum(dmixed * tap_rows(k), axis=0, keepdims=True)
+        for c in range(CHUNKS):
+            tap_part[c, k : k + 1, :] = term[:, c * LANES : (c + 1) * LANES]
+    tap_copies = [
+        remote(tap_part.at[c], tap_in.at[me], tap_s.at[c], tap_r.at[me], c) for c in range(CHUNKS)
+    ]
+    for c in range(CHUNKS):
+        pl.when(me != c)(tap_copies[c].start)
+
+    natural = one_hot(row, tile_of_lane)
+    attended_ref[...] = bf16_dot(natural, out_perm).astype(jnp.bfloat16)
+    own_back = bf16_dot(back_own[...], split[...])
+    total = own_back[(KERNEL // 2) * ROWS : (KERNEL // 2 + 1) * ROWS]
+    for k in range(KERNEL):
+        j = KERNEL - 1 - k
+        total = total + conv_ref[k : k + 1, :] * own_back[j * ROWS : (j + 1) * ROWS]
+
+    @pl.when(me < CHUNKS)
+    def _():
+        tap_in[me] = tap_part[me]
+
+        @pl.loop(1, n)
+        def _(step):
+            peer = lax.rem(me + n - step, n)
+            remote(tap_part.at[0], tap_in.at[peer], tap_s.at[0], tap_r.at[peer], peer).wait_recv()
+
+        tap_all[me] = jnp.sum(tap_in[...], axis=0)
+
+        @pl.loop(1, n)
+        def _(step):
+            peer = lax.rem(me + step, n)
+            remote(tap_all.at[me], tap_all.at[me], all_s.at[peer], all_r.at[me], peer).start()
+
+    arrive_exchange(back_copies)
+    halo_back = bf16_dot(back_halo[...], back_rows[...])
+    for k in range(KERNEL):
+        j = KERNEL - 1 - k
+        total = total + conv_ref[k : k + 1, :] * halo_back[j * ROWS : (j + 1) * ROWS]
+    tiles_ref[...] = total.astype(jnp.bfloat16)
+
+    for c in range(CHUNKS):
+        pl.when(me != c)(
+            remote(tap_all.at[c], tap_all.at[c], all_s.at[c], all_r.at[c], c).wait_recv
+        )
+    for c in range(CHUNKS):
+        taps_ref[:, c * LANES : (c + 1) * LANES] = tap_all[c, 0:KERNEL, :]
+
+    finish_exchange(tile_copies)
+    finish_all_to_all(heads_out, heads_in, heads_s, heads_r)
+    finish_all_to_all(grads_out, grads_in, grads_s, grads_r)
+    finish_exchange(back_copies)
+    for c in range(CHUNKS):
+        pl.when(me != c)(tap_copies[c].wait_send)
+
+    @pl.when(me < CHUNKS)
+    def _():
+        @pl.loop(1, n)
+        def _(step):
+            peer = lax.rem(me + step, n)
+            remote(tap_all.at[me], tap_all.at[me], all_s.at[peer], all_r.at[me], peer).wait_send()
+
+
+def per_device_heads(n, tile_embed, grad_output, query_key_value_weight, conv_weight, neighbours):
+    bf16, f32, i32 = jnp.bfloat16, jnp.float32, jnp.int32
+    taps = KERNEL * ROWS
+    dma = pltpu.SemaphoreType.DMA
+    vmem = pl.BlockSpec(memory_space=pltpu.VMEM)
+    return pl.pallas_call(
+        functools.partial(slide_kernel, n),
+        out_shape=(
+            jax.ShapeDtypeStruct((ROWS, MODEL_WIDTH), bf16),
+            jax.ShapeDtypeStruct((ROWS, MODEL_WIDTH), bf16),
+            jax.ShapeDtypeStruct((KERNEL, MODEL_WIDTH), f32),
+        ),
+        in_specs=[vmem, vmem, pl.BlockSpec(memory_space=pl.ANY), vmem, vmem],
+        out_specs=(vmem, vmem, vmem),
+        scratch_shapes=[
+            pltpu.VMEM(query_key_value_weight.shape, bf16),
+            pltpu.VMEM((LANES, ROWS), i32),
+            pltpu.VMEM((ROWS, LANES), i32),
+            pltpu.VMEM((ROWS, LANES), i32),
+            pltpu.VMEM((2 * ROWS, MODEL_WIDTH), bf16),
+            pltpu.VMEM((taps, MODEL_WIDTH), f32),
+            pltpu.VMEM((taps, MODEL_WIDTH), bf16),
+            pltpu.VMEM((taps, ROWS), bf16),
+            pltpu.VMEM((taps, 2 * ROWS), bf16),
+            pltpu.VMEM((taps, 2 * ROWS), bf16),
+            pltpu.VMEM((taps, 2 * ROWS), bf16),
+            pltpu.VMEM((ROWS, MODEL_WIDTH), bf16),
+            pltpu.VMEM((n, PACKED, LANES), bf16),
+            pltpu.VMEM((n, PACKED, LANES), bf16),
+            pltpu.VMEM((n, PACKED, LANES), bf16),
+            pltpu.VMEM((n, PACKED, LANES), bf16),
+            pltpu.VMEM((2 * ROWS, MODEL_WIDTH), bf16),
+            pltpu.VMEM((2 * ROWS, MODEL_WIDTH), bf16),
+            pltpu.VMEM((CHUNKS, 16, LANES), f32),
+            pltpu.VMEM((n, 16, LANES), f32),
+            pltpu.VMEM((CHUNKS, 16, LANES), f32),
+            dma,
+            dma((2,)),
+            dma((2,)),
+            dma((n,)),
+            dma((n,)),
+            dma((n,)),
+            dma((n,)),
+            dma((2,)),
+            dma((2,)),
+            dma((CHUNKS,)),
+            dma((n,)),
+            dma((n,)),
+            dma((CHUNKS,)),
+        ],
+        compiler_params=pltpu.CompilerParams(
+            collective_id=0, has_side_effects=True, vmem_limit_bytes=VMEM_BYTES
+        ),
+    )(tile_embed, grad_output, query_key_value_weight, conv_weight, neighbours)
+
+
+def per_device_choice(n, tile_embed, *rest):
+    if n == HEAD_COUNT and tile_embed.shape[0] == ROWS:
+        return per_device_heads(n, tile_embed, *rest)
+    return per_device(tile_embed, *rest)
+
+
 def solution(mesh):
     placed = (
         P(("slide", "seq"), None),
@@ -231,7 +628,7 @@
         P(None, ("slide", "seq")),
     )
     return jax.shard_map(
-        per_device,
+        functools.partial(per_device_choice, mesh.shape["seq"]),
         mesh=mesh,
         in_specs=placed,
         out_specs=(P(("slide", "seq"), None), P(("slide", "seq"), None), P("slide", None)),

time: 432 us -> 47.2 us (0.11); the launches traced: 424 us -> 46.9 us
  blocking collectives: 183 us -> 0 us
  matrix products: 141 us -> 0 us
  other arithmetic: 43.9 us -> 0 us
  Pallas kernels: 0 us -> 41.6 us
  local copies, waits for them, and re-layouts: 45.1 us -> 4.65 us
  starting transfers between devices: 9.32 us -> 0 us
    dot_general x104 -> x0, matrix products: 141 us -> none  [the longest x32 51.4 us: contract_first(): lax.dot_general(left, right, (((0,), (0,)), ((), ())), preferred_element_...]
    all_gather x6 -> x0, blocking collectives: 123 us -> none  [the longest x1 25.6 us: per_device(): dout_piece = lax.all_gather(dout_sel, 'seq', axis=0, tiled=True)]
    psum x1 -> x0, blocking collectives: 59.7 us -> none  [per_device(): grad_conv = lax.psum(conv_terms, 'seq')]
    pallas_call x0 -> x1, Pallas kernels: none -> 41.6 us  [per_device_heads(): pl.pallas_call(functools.partial(slide_kernel, n), out_shape=(jax.ShapeDt...]
    scatter-add x9 -> x0, other arithmetic: 18.5 us -> none  [per_device(): contrib.at[local_index[k]]]
    reduce_sum x33 -> x0, other arithmetic: 17.7 us -> none  [the longest x16 12.9 us: head_forward(): jnp.sum(douts.astype(jnp.float32) * output.astype(jnp.float32), axis=1)]
    slice x14 -> x0, local copies, waits for them, and re-layouts: 14.1 us -> none  [the longest x3 4.42 us: per_device(): group_index.reshape(partial_rows, each_group, DILATION_STEP, HEAD_SIZE)]
    ppermute x4 -> x0, starting transfers between devices: 9.32 us -> none  [the longest x2 4.31 us: from_behind(): lax.ppermute(value, axis, [(source, source + steps) for source in range(l...]
  transfers between devices with their start and end apart: 4 -> 0, of which waited for: 0 -> 0; matrix products, arithmetic and copies ran while one was open for 4% -> 0% of each run, Pallas kernels for 0% -> 0%
where the time goes in v1:
time: 47.2 us; the launch traced here: 46.9 us
  Pallas kernels  41.6 us (88%)
  local copies, waits for them, and re-layouts  4.65 us (10%)
  between operations  0.64 us (1%)
    pallas_call x1, Pallas kernels, per_device_heads(): pl.pallas_call(functools.partial(slide_kernel, n), out_shape=(jax.ShapeDt...  41.6 us
    unnamed x3, local copies, waits for them, and re-layouts  4.65 us

profile of v1, /device:TPU:0, one launch (start us, length us, event | category | flops | bytes accessed | tf_op | source)
XLA Modules:
  0.0 46.9 jit_solution(12240514603355717950)
XLA Ops:
  0.6 41.6 %shard_map.76 = (bf16[128,768]{1,0:T(8,128)(2,1)}, bf16[128,768]{1,0:T(8,128)(2,1)}, f32[9,768]{1,0:T(8,128)}) custom-call(bf16[128,768]{1,0:T(8,128)(2,1)} %tile_ref.1, bf16[128,768]{1,0:T(8,128)(2,1)} %dout_ref.1, bf16[768,2304]{1,0:T(8,128)(2,1)} %weight_hbm.1, f32[9,768]{1,0:T(8,128)} %conv_ref.1, s32[9,128]{1,0:T(8,128)} %near_ref.1), custom_call_target="tpu_custom_call" | custom-call | tf_op jit(solution)/shard_map/pallas_call | solution.py:565
  42.3 1.6 %copy.11 = bf16[128,768]{1,0:T(8,128)(2,1)} copy(bf16[128,768]{1,0:T(8,128)(2,1)} %get-tuple-element.6) | data formatting | bytes 393216
  43.9 1.6 %copy.12 = bf16[128,768]{1,0:T(8,128)(2,1)} copy(bf16[128,768]{1,0:T(8,128)(2,1)} %get-tuple-element.7) | data formatting | bytes 393216
  45.5 1.4 %copy.13 = f32[9,768]{1,0:T(8,128)} copy(f32[9,768]{1,0:T(8,128)} %get-tuple-element.8) | data formatting | bytes 55296

commit v2 on v1

--- a/solution.py
+++ b/solution.py
@@ -407,7 +407,7 @@
     def all_to_all(source, target, send_sem, recv_sem):
         @pl.loop(1, n)
         def _(step):
-            peer = lax.rem(me + step, n)
+            peer = me ^ (n - step)
             remote(
                 source.at[peer], target.at[me], send_sem.at[peer], recv_sem.at[me], peer
             ).start()
@@ -491,7 +491,6 @@
     split[0:ROWS, :] = high
     split[ROWS : 2 * ROWS, :] = (dmixed - high.astype(jnp.float32)).astype(jnp.bfloat16)
     back_copies = exchange(split.at[pl.ds(0, ROWS)], back_rows, back_s, back_r)
-    start_exchange(back_copies)
 
     tap_part[...] = jnp.zeros_like(tap_part)
     for k in range(KERNEL):
@@ -503,6 +502,7 @@
     ]
     for c in range(CHUNKS):
         pl.when(me != c)(tap_copies[c].start)
+    start_exchange(back_copies)
 
     natural = one_hot(row, tile_of_lane)
     attended_ref[...] = bf16_dot(natural, out_perm).astype(jnp.bfloat16)
@@ -613,9 +613,25 @@
     )(tile_embed, grad_output, query_key_value_weight, conv_weight, neighbours)
 
 
+def hand_on_kernel(a_ref, b_ref, c_ref, a_out, b_out, c_out):
+    a_out[...] = a_ref[...]
+    b_out[...] = b_ref[...]
+    c_out[...] = c_ref[...]
+
+
+def hand_on(*arrays):
+    vmem = pl.BlockSpec(memory_space=pltpu.VMEM)
+    return pl.pallas_call(
+        hand_on_kernel,
+        out_shape=tuple(jax.ShapeDtypeStruct(x.shape, x.dtype) for x in arrays),
+        in_specs=[vmem] * 3,
+        out_specs=(vmem,) * 3,
+    )(*arrays)
+
+
 def per_device_choice(n, tile_embed, *rest):
     if n == HEAD_COUNT and tile_embed.shape[0] == ROWS:
-        return per_device_heads(n, tile_embed, *rest)
+        return hand_on(*per_device_heads(n, tile_embed, *rest))
     return per_device(tile_embed, *rest)
 
 

time: 47.2 us -> 41.3 us (0.87)
  local copies, waits for them, and re-layouts: 4.65 us -> 0 us
  Pallas kernels: 41.6 us -> 40.5 us
    unnamed x3 -> x0, local copies, waits for them, and re-layouts: 4.65 us -> none
    pallas_call x1, Pallas kernels: 41.6 us -> 38.7 us  [per_device_heads(): pl.pallas_call(functools.partial(slide_kernel, n), out_shape=(jax.ShapeDt...]
    pallas_call x0 -> x1, Pallas kernels: none -> 1.79 us  [hand_on(): pl.pallas_call(hand_on_kernel, out_shape=tuple((jax.ShapeDtypeStruct(x.sh...]
where the time goes in v2:
time: 41.3 us; the launch traced here: 41.1 us
  Pallas kernels  40.5 us (98%)
  between operations  0.64 us (2%)
    pallas_call x1, Pallas kernels, per_device_heads(): pl.pallas_call(functools.partial(slide_kernel, n), out_shape=(jax.ShapeDt...  38.7 us
    pallas_call x1, Pallas kernels, hand_on(): pl.pallas_call(hand_on_kernel, out_shape=tuple((jax.ShapeDtypeStruct(x.sh...  1.79 us

profile of v2, /device:TPU:0, one launch (start us, length us, event | category | flops | bytes accessed | tf_op | source)
XLA Modules:
  0.0 41.1 jit_solution(1011235396899203722)
XLA Ops:
  0.6 38.7 %shard_map.76 = (bf16[128,768]{1,0:T(8,128)(2,1)}, bf16[128,768]{1,0:T(8,128)(2,1)}, f32[9,768]{1,0:T(8,128)}) custom-call(bf16[128,768]{1,0:T(8,128)(2,1)} %tile_ref.1, bf16[128,768]{1,0:T(8,128)(2,1)} %dout_ref.1, bf16[768,2304]{1,0:T(8,128)(2,1)} %weight_hbm.1, f32[9,768]{1,0:T(8,128)} %conv_ref.1, s32[9,128]{1,0:T(8,128)} %near_ref.1), custom_call_target="tpu_custom_call" | custom-call | tf_op jit(solution)/shard_map/pallas_call | solution.py:565
  39.3 1.8 %shard_map.77 = (bf16[128,768]{1,0:T(8,128)(2,1)}, bf16[128,768]{1,0:T(8,128)(2,1)}, f32[9,768]{1,0:T(8,128)}) custom-call(bf16[128,768]{1,0:T(8,128)(2,1)} %get-tuple-element.6.a_ref, bf16[128,768]{1,0:T(8,128)(2,1)} %get-tuple-element.7.b_ref, f32[9,768]{1,0:T(8,128)} %get-tuple-element.8.c_ref), custom_call_target="tpu_custom_call" | custom-call | tf_op jit(solution)/shard_map/pallas_call | solution.py:624

commit v3 on v2

--- a/solution.py
+++ b/solution.py
@@ -404,30 +404,23 @@
         heads_out[h, PART:PACKED, 0:16] = v[0:16, 32:48]
         heads_out[h, PART:PACKED, 16:32] = v[16:32, 32:48]
 
+    other = lax.rem(me + 1, n)
+
+    def whole(source, target, send_sem, recv_sem):
+        most = pl.ds(0, n - 1)
+        return remote(source.at[most], target.at[most], send_sem, recv_sem, other)
+
     def all_to_all(source, target, send_sem, recv_sem):
         @pl.loop(1, n)
         def _(step):
             peer = me ^ (n - step)
-            remote(
-                source.at[peer], target.at[me], send_sem.at[peer], recv_sem.at[me], peer
-            ).start()
+            remote(source.at[peer], target.at[me], send_sem, recv_sem, peer).start()
 
         target[me] = source[me]
-
-        @pl.loop(1, n)
-        def _(step):
-            peer = lax.rem(me + n - step, n)
-            remote(
-                source.at[peer], target.at[peer], send_sem.at[peer], recv_sem.at[peer], peer
-            ).wait_recv()
+        whole(source, target, send_sem, recv_sem).wait_recv()
 
     def finish_all_to_all(source, target, send_sem, recv_sem):
-        @pl.loop(1, n)
-        def _(step):
-            peer = lax.rem(me + step, n)
-            remote(
-                source.at[peer], target.at[me], send_sem.at[peer], recv_sem.at[me], peer
-            ).wait_send()
+        whole(source, target, send_sem, recv_sem).wait_send()
 
     all_to_all(heads_out, heads_in, heads_s, heads_r)
 
@@ -498,7 +491,7 @@
         for c in range(CHUNKS):
             tap_part[c, k : k + 1, :] = term[:, c * LANES : (c + 1) * LANES]
     tap_copies = [
-        remote(tap_part.at[c], tap_in.at[me], tap_s.at[c], tap_r.at[me], c) for c in range(CHUNKS)
+        remote(tap_part.at[c], tap_in.at[me], tap_s.at[c], tap_r, c) for c in range(CHUNKS)
     ]
     for c in range(CHUNKS):
         pl.when(me != c)(tap_copies[c].start)
@@ -516,18 +509,18 @@
     def _():
         tap_in[me] = tap_part[me]
 
-        @pl.loop(1, n)
-        def _(step):
-            peer = lax.rem(me + n - step, n)
-            remote(tap_part.at[0], tap_in.at[peer], tap_s.at[0], tap_r.at[peer], peer).wait_recv()
+        whole(tap_in, tap_in, all_s, tap_r).wait_recv()
 
         tap_all[me] = jnp.sum(tap_in[...], axis=0)
 
         @pl.loop(1, n)
         def _(step):
             peer = lax.rem(me + step, n)
-            remote(tap_all.at[me], tap_all.at[me], all_s.at[peer], all_r.at[me], peer).start()
-
+            remote(tap_all.at[me], tap_all.at[me], all_s, all_r.at[me], peer).start()
+
+    finish_exchange(tile_copies)
+    finish_all_to_all(heads_out, heads_in, heads_s, heads_r)
+    finish_all_to_all(grads_out, grads_in, grads_s, grads_r)
     arrive_exchange(back_copies)
     halo_back = bf16_dot(back_halo[...], back_rows[...])
     for k in range(KERNEL):
@@ -537,24 +530,18 @@
 
     for c in range(CHUNKS):
         pl.when(me != c)(
-            remote(tap_all.at[c], tap_all.at[c], all_s.at[c], all_r.at[c], c).wait_recv
+            remote(tap_all.at[c], tap_all.at[c], all_s, all_r.at[c], c).wait_recv
         )
     for c in range(CHUNKS):
         taps_ref[:, c * LANES : (c + 1) * LANES] = tap_all[c, 0:KERNEL, :]
 
-    finish_exchange(tile_copies)
-    finish_all_to_all(heads_out, heads_in, heads_s, heads_r)
-    finish_all_to_all(grads_out, grads_in, grads_s, grads_r)
     finish_exchange(back_copies)
     for c in range(CHUNKS):
         pl.when(me != c)(tap_copies[c].wait_send)
 
     @pl.when(me < CHUNKS)
     def _():
-        @pl.loop(1, n)
-        def _(step):
-            peer = lax.rem(me + step, n)
-            remote(tap_all.at[me], tap_all.at[me], all_s.at[peer], all_r.at[me], peer).wait_send()
+        whole(tap_in, tap_in, all_s, tap_r).wait_send()
 
 
 def per_device_heads(n, tile_embed, grad_output, query_key_value_weight, conv_weight, neighbours):
@@ -596,15 +583,15 @@
             dma,
             dma((2,)),
             dma((2,)),
-            dma((n,)),
-            dma((n,)),
-            dma((n,)),
-            dma((n,)),
+            dma,
+            dma,
+            dma,
+            dma,
             dma((2,)),
             dma((2,)),
             dma((CHUNKS,)),
-            dma((n,)),
-            dma((n,)),
+            dma,
+            dma,
             dma((CHUNKS,)),
         ],
         compiler_params=pltpu.CompilerParams(

time: 41.3 us -> 40 us (0.969)
  Pallas kernels: 40.5 us -> 39.2 us
    pallas_call x1, Pallas kernels: 38.7 us -> 37.5 us  [per_device_heads(): pl.pallas_call(functools.partial(slide_kernel, n), out_shape=(jax.ShapeDt...]
where the time goes in v3:
time: 40 us; the launch traced here: 39.9 us
  Pallas kernels  39.2 us (98%)
  between operations  0.64 us (2%)
    pallas_call x1, Pallas kernels, per_device_heads(): pl.pallas_call(functools.partial(slide_kernel, n), out_shape=(jax.ShapeDt...  37.5 us
    pallas_call x1, Pallas kernels, hand_on(): pl.pallas_call(hand_on_kernel, out_shape=tuple((jax.ShapeDtypeStruct(x.sh...  1.79 us

profile of v3, /device:TPU:0, one launch (start us, length us, event | category | flops | bytes accessed | tf_op | source)
XLA Modules:
  0.0 39.9 jit_solution(13900838565688951285)
XLA Ops:
  0.6 37.5 %shard_map.76 = (bf16[128,768]{1,0:T(8,128)(2,1)}, bf16[128,768]{1,0:T(8,128)(2,1)}, f32[9,768]{1,0:T(8,128)}) custom-call(bf16[128,768]{1,0:T(8,128)(2,1)} %tile_ref.1, bf16[128,768]{1,0:T(8,128)(2,1)} %dout_ref.1, bf16[768,2304]{1,0:T(8,128)(2,1)} %weight_hbm.1, f32[9,768]{1,0:T(8,128)} %conv_ref.1, s32[9,128]{1,0:T(8,128)} %near_ref.1), custom_call_target="tpu_custom_call" | custom-call | tf_op jit(solution)/shard_map/pallas_call | solution.py:552
  38.1 1.8 %shard_map.77 = (bf16[128,768]{1,0:T(8,128)(2,1)}, bf16[128,768]{1,0:T(8,128)(2,1)}, f32[9,768]{1,0:T(8,128)}) custom-call(bf16[128,768]{1,0:T(8,128)(2,1)} %get-tuple-element.6.a_ref, bf16[128,768]{1,0:T(8,128)(2,1)} %get-tuple-element.7.b_ref, f32[9,768]{1,0:T(8,128)} %get-tuple-element.8.c_ref), custom_call_target="tpu_custom_call" | custom-call | tf_op jit(solution)/shard_map/pallas_call | solution.py:611

commit v4 on v3

--- a/solution.py
+++ b/solution.py
@@ -255,11 +255,11 @@
 
 def slide_kernel(
     n,
-    tile_ref,
-    dout_ref,
+    tile_hbm,
+    dout_hbm,
     weight_hbm,
-    conv_ref,
-    near_ref,
+    conv_hbm,
+    near_hbm,
     attended_ref,
     tiles_ref,
     taps_ref,
@@ -297,10 +297,25 @@
     tap_r,
     all_s,
     all_r,
+    tile_ref,
+    dout_ref,
+    conv_ref,
+    near_ref,
+    load_s,
 ):
     me = lax.axis_index("seq")
     load_weight = pltpu.make_async_copy(weight_hbm, weight, weight_sem)
-    load_weight.start()
+    loads = [
+        pltpu.make_async_copy(source, target, load_s.at[i])
+        for i, (source, target) in enumerate(
+            (
+                (near_hbm, near_ref),
+                (dout_hbm, dout_ref),
+                (tile_hbm, tile_ref),
+                (conv_hbm, conv_ref),
+            )
+        )
+    ]
 
     barrier = pltpu.get_barrier_semaphore()
 
@@ -312,6 +327,12 @@
             device_id={"seq": lax.rem(me + step, n)},
             device_id_type=pl.DeviceIdType.MESH,
         )
+
+    for load in loads:
+        load.start()
+    load_weight.start()
+    for load in loads:
+        load.wait()
 
     near = near_ref[...]
     near_pad[...] = jnp.full((LANES, ROWS), -1, jnp.int32)
@@ -497,6 +518,19 @@
         pl.when(me != c)(tap_copies[c].start)
     start_exchange(back_copies)
 
+    @pl.when(me < CHUNKS)
+    def _():
+        tap_in[me] = tap_part[me]
+
+        whole(tap_in, tap_in, all_s, tap_r).wait_recv()
+
+        tap_all[me] = jnp.sum(tap_in[...], axis=0)
+
+        @pl.loop(1, n)
+        def _(step):
+            peer = lax.rem(me + step, n)
+            remote(tap_all.at[me], tap_all.at[me], all_s, all_r.at[me], peer).start()
+
     natural = one_hot(row, tile_of_lane)
     attended_ref[...] = bf16_dot(natural, out_perm).astype(jnp.bfloat16)
     own_back = bf16_dot(back_own[...], split[...])
@@ -504,19 +538,6 @@
     for k in range(KERNEL):
         j = KERNEL - 1 - k
         total = total + conv_ref[k : k + 1, :] * own_back[j * ROWS : (j + 1) * ROWS]
-
-    @pl.when(me < CHUNKS)
-    def _():
-        tap_in[me] = tap_part[me]
-
-        whole(tap_in, tap_in, all_s, tap_r).wait_recv()
-
-        tap_all[me] = jnp.sum(tap_in[...], axis=0)
-
-        @pl.loop(1, n)
-        def _(step):
-            peer = lax.rem(me + step, n)
-            remote(tap_all.at[me], tap_all.at[me], all_s, all_r.at[me], peer).start()
 
     finish_exchange(tile_copies)
     finish_all_to_all(heads_out, heads_in, heads_s, heads_r)
@@ -556,7 +577,7 @@
             jax.ShapeDtypeStruct((ROWS, MODEL_WIDTH), bf16),
             jax.ShapeDtypeStruct((KERNEL, MODEL_WIDTH), f32),
         ),
-        in_specs=[vmem, vmem, pl.BlockSpec(memory_space=pl.ANY), vmem, vmem],
+        in_specs=[pl.BlockSpec(memory_space=pl.ANY)] * 5,
         out_specs=(vmem, vmem, vmem),
         scratch_shapes=[
             pltpu.VMEM(query_key_value_weight.shape, bf16),
@@ -577,9 +598,9 @@
             pltpu.VMEM((n, PACKED, LANES), bf16),
             pltpu.VMEM((2 * ROWS, MODEL_WIDTH), bf16),
             pltpu.VMEM((2 * ROWS, MODEL_WIDTH), bf16),
-            pltpu.VMEM((CHUNKS, 16, LANES), f32),
-            pltpu.VMEM((n, 16, LANES), f32),
-            pltpu.VMEM((CHUNKS, 16, LANES), f32),
+            pltpu.VMEM((CHUNKS, KERNEL, LANES), f32),
+            pltpu.VMEM((n, KERNEL, LANES), f32),
+            pltpu.VMEM((CHUNKS, KERNEL, LANES), f32),
             dma,
             dma((2,)),
             dma((2,)),
@@ -593,6 +614,11 @@
             dma,
             dma,
             dma((CHUNKS,)),
+            pltpu.VMEM((ROWS, MODEL_WIDTH), bf16),
+            pltpu.VMEM((ROWS, MODEL_WIDTH), bf16),
+            pltpu.VMEM((KERNEL, MODEL_WIDTH), f32),
+            pltpu.VMEM((KERNEL, ROWS), i32),
+            dma((4,)),
         ],
         compiler_params=pltpu.CompilerParams(
             collective_id=0, has_side_effects=True, vmem_limit_bytes=VMEM_BYTES

time: 40 us -> 38.8 us (0.970)
  Pallas kernels: 39.2 us -> 37.9 us
    pallas_call x1, Pallas kernels: 37.5 us -> 36.1 us  [per_device_heads(): pl.pallas_call(functools.partial(slide_kernel, n), out_shape=(jax.ShapeDt...]
where the time goes in v4:
time: 38.8 us; the launch traced here: 38.6 us
  Pallas kernels  37.9 us (98%)
  between operations  0.64 us (2%)
    pallas_call x1, Pallas kernels, per_device_heads(): pl.pallas_call(functools.partial(slide_kernel, n), out_shape=(jax.ShapeDt...  36.1 us
    pallas_call x1, Pallas kernels, hand_on(): pl.pallas_call(hand_on_kernel, out_shape=tuple((jax.ShapeDtypeStruct(x.sh...  1.79 us

profile of v4, /device:TPU:0, one launch (start us, length us, event | category | flops | bytes accessed | tf_op | source)
XLA Modules:
  0.0 38.6 jit_solution(18062089816512603171)
XLA Ops:
  0.6 36.1 %shard_map.76 = (bf16[128,768]{1,0:T(8,128)(2,1)}, bf16[128,768]{1,0:T(8,128)(2,1)}, f32[9,768]{1,0:T(8,128)}) custom-call(bf16[128,768]{1,0:T(8,128)(2,1)} %tile_hbm.1, bf16[128,768]{1,0:T(8,128)(2,1)} %dout_hbm.1, bf16[768,2304]{1,0:T(8,128)(2,1)} %weight_hbm.1, f32[9,768]{1,0:T(8,128)} %conv_hbm.1, s32[9,128]{1,0:T(8,128)} %near_hbm.1), custom_call_target="tpu_custom_call" | custom-call | tf_op jit(solution)/shard_map/pallas_call | solution.py:573
  36.8 1.8 %shard_map.77 = (bf16[128,768]{1,0:T(8,128)(2,1)}, bf16[128,768]{1,0:T(8,128)(2,1)}, f32[9,768]{1,0:T(8,128)}) custom-call(bf16[128,768]{1,0:T(8,128)(2,1)} %get-tuple-element.6.a_ref, bf16[128,768]{1,0:T(8,128)(2,1)} %get-tuple-element.7.b_ref, f32[9,768]{1,0:T(8,128)} %get-tuple-element.8.c_ref), custom_call_target="tpu_custom_call" | custom-call | tf_op jit(solution)/shard_map/pallas_call | solution.py:637
